TPU v7x, 32 devices: a whole 2x2x4 slice. The times are simulated.
32 devices in a mesh: seq: 8 (over z, x), ch: 4 (over y, core).
Axes of the slice: x: 2, y: 2, z: 4, core: 2. Of those that a mesh axis runs over, the one named last changes fastest.
Arguments:
- block_input: bfloat16 [8192, 2048], P('ch', 'seq'), may hold values from -110 to 110
- norm_gain: float32 [8192], P('ch'), may hold values from 0.1 to 1.9
- short_taps: bfloat16 [8192, 7], P('ch'), may hold values from -2 to 2
- medium_taps: bfloat16 [8192, 128], P('ch'), may hold values from -0.5 to 0.5
- long_filter: float32 [8192, 2048], P(('ch', 'seq')), may hold values from -2 to 2
- grad_out: bfloat16 [8192, 2048], P('ch', 'seq'), may hold values from -2.390625 to 2.390625
Outputs:
- grad_normed: bfloat16 [8192, 2048], P('ch', 'seq')
- grad_long: float32 [8192, 2048], P(('ch', 'seq'))
- grad_medium: float32 [8192, 128], P(('ch', 'seq'))
- grad_short: float32 [8192, 7], P(('ch', 'seq'))
All inputs are finite; a program needn't handle non-finite values.
Results may differ from a plain program's by a relative error of at most 0.0058.
Values may be sent and summed in bfloat16 or wider, within the bound.
A program may use at most 128 MiB of HBM per device.

v0:
```python
import math
import jax
import jax.numpy as jnp
from jax import lax
from jax.sharding import PartitionSpec as P

highest = lax.Precision.HIGHEST


def depthwise(signal, taps):
    result = lax.conv_general_dilated(
        signal[None],
        taps[:, None, :],
        (1,),
        "VALID",
        dimension_numbers=("NCH", "OIH", "NCH"),
        feature_group_count=signal.shape[0],
        preferred_element_type=jnp.float32,
    )
    return result[0]


def fourier_tables(length):
    total = 2 * length
    inner = 128
    outer = total // inner
    half = outer // 2
    two_pi = 2.0 * math.pi
    freq_outer = jnp.arange(outer, dtype=jnp.int32)
    pos_half = jnp.arange(half, dtype=jnp.int32)
    pos_inner = jnp.arange(inner, dtype=jnp.int32)
    outer_angle = (
        two_pi * (freq_outer[:, None] * pos_half[None, :] % outer).astype(jnp.float32) / outer
    )
    inner_angle = (
        two_pi * (pos_inner[:, None] * pos_inner[None, :] % inner).astype(jnp.float32) / inner
    )
    twist_angle = (
        two_pi * (freq_outer[:, None] * pos_inner[None, :] % total).astype(jnp.float32) / total
    )
    return (
        jnp.cos(outer_angle),
        jnp.sin(outer_angle),
        jnp.cos(inner_angle),
        jnp.sin(inner_angle),
        jnp.cos(twist_angle),
        jnp.sin(twist_angle),
    )


def forward_dft(signal, tables):
    cos_outer, sin_outer, cos_inner, sin_inner, cos_twist, sin_twist = tables
    blocks = signal.reshape(signal.shape[0], cos_outer.shape[1], cos_inner.shape[0])
    real = jnp.einsum("kn,cnq->ckq", cos_outer, blocks, precision=highest)
    imag = -jnp.einsum("kn,cnq->ckq", sin_outer, blocks, precision=highest)
    turned_re = real * cos_twist + imag * sin_twist
    turned_im = imag * cos_twist - real * sin_twist
    out_re = jnp.einsum("ckq,qr->ckr", turned_re, cos_inner, precision=highest) + jnp.einsum(
        "ckq,qr->ckr", turned_im, sin_inner, precision=highest
    )
    out_im = jnp.einsum("ckq,qr->ckr", turned_im, cos_inner, precision=highest) - jnp.einsum(
        "ckq,qr->ckr", turned_re, sin_inner, precision=highest
    )
    return (out_re, out_im)


def inverse_dft(spec_re, spec_im, tables):
    cos_outer, sin_outer, cos_inner, sin_inner, cos_twist, sin_twist = tables
    total = cos_outer.shape[0] * cos_inner.shape[0]
    step_re = jnp.einsum("ckq,qr->ckr", spec_re, cos_inner, precision=highest) - jnp.einsum(
        "ckq,qr->ckr", spec_im, sin_inner, precision=highest
    )
    step_im = jnp.einsum("ckq,qr->ckr", spec_im, cos_inner, precision=highest) + jnp.einsum(
        "ckq,qr->ckr", spec_re, sin_inner, precision=highest
    )
    turned_re = step_re * cos_twist - step_im * sin_twist
    turned_im = step_im * cos_twist + step_re * sin_twist
    blocks = jnp.einsum("kn,ckq->cnq", cos_outer, turned_re, precision=highest) - jnp.einsum(
        "kn,ckq->cnq", sin_outer, turned_im, precision=highest
    )
    return (blocks / total).reshape(spec_re.shape[0], -1)


def on_device(block_input, norm_gain, short_taps, medium_taps, long_filter, grad_out):
    chans, tokens = block_input.shape
    seq_count = lax.axis_size("seq")
    med_count = medium_taps.shape[1]
    reach = med_count + short_taps.shape[1] - 2
    inputs32 = block_input.astype(jnp.float32)
    squares = lax.psum(jnp.sum(inputs32 * inputs32, axis=0), "ch")
    inv_rms = lax.rsqrt(squares / (chans * lax.axis_size("ch")) + 1e-05)
    normed = (inputs32 * inv_rms[None, :] * norm_gain[:, None]).astype(jnp.bfloat16)
    arrived, grad_chan = (
        lax.all_to_all(normed, "seq", split_axis=0, concat_axis=1, tiled=True),
        lax.all_to_all(grad_out, "seq", split_axis=0, concat_axis=1, tiled=True),
    )
    group, length = arrived.shape
    scale = length ** (-0.5)
    offset = lax.axis_index("seq") * group
    short_local = lax.dynamic_slice_in_dim(short_taps, offset, group, 0)
    medium_local = lax.dynamic_slice_in_dim(medium_taps, offset, group, 0)
    normed_pad = jnp.pad(arrived, ((0, 0), (reach, 0)))
    shorted_pad = depthwise(normed_pad, short_local[:, ::-1]).astype(jnp.bfloat16)
    filtered_chan = depthwise(shorted_pad, medium_local[:, ::-1]).astype(jnp.bfloat16)
    tables = fourier_tables(length)
    grad_re, grad_im = forward_dft(grad_chan.astype(jnp.float32), tables)
    filt_re, filt_im = forward_dft(long_filter, tables)
    sig_re, sig_im = forward_dft(filtered_chan.astype(jnp.float32), tables)
    grad_filtered = inverse_dft(
        filt_re * grad_re + filt_im * grad_im, filt_re * grad_im - filt_im * grad_re, tables
    ).astype(jnp.bfloat16)
    grad_long = (
        inverse_dft(
            sig_re * grad_re + sig_im * grad_im, sig_re * grad_im - sig_im * grad_re, tables
        )
        * scale
    )
    back_pad = jnp.pad(grad_filtered, ((0, 0), (0, reach)))
    shorted_grad = depthwise(back_pad, medium_local).astype(jnp.bfloat16)
    normed_grad = depthwise(shorted_grad, short_local).astype(jnp.bfloat16)
    medium_local_grad = depthwise(shorted_pad, grad_filtered)[:, ::-1] * scale
    short_local_grad = (
        depthwise(normed_pad[:, med_count - 1 :], shorted_grad[:, :length])[:, ::-1] * scale
    )
    leaving = normed_grad.reshape(group, seq_count, tokens)
    returned = lax.all_to_all(leaving, "seq", split_axis=1, concat_axis=0, tiled=True).reshape(
        chans, -1
    )
    return (returned, grad_long, medium_local_grad, short_local_grad)


def solution(mesh):
    placed = (
        P("ch", "seq"),
        P("ch"),
        P("ch", None),
        P("ch", None),
        P(("ch", "seq"), None),
        P("ch", "seq"),
    )
    return jax.shard_map(
        on_device,
        mesh=mesh,
        in_specs=placed,
        out_specs=(
            P("ch", "seq"),
            P(("ch", "seq"), None),
            P(("ch", "seq"), None),
            P(("ch", "seq"), None),
        ),
        check_vma=False,
    )
```

profile of v0, /device:TPU:0, one launch (start us, length us, event | category | flops | bytes accessed | tf_op | source)
XLA Modules:
  0.0 433.6 jit_solution(14907793232586408200)
XLA Ops:
  2.2 8.4 %psum.7 = f32[256]{0:T(256)S(1)} all-reduce(f32[256]{0:T(256)S(1)} %fusion.44), channel_id=1, replica_groups=mesh['seq'=8,'ch'=4] {'ch'}, use_global_device_ids=true, to_apply=%region_1.0 | all-reduce | flops 256 | bytes 2048 | tf_op jit(solution)/shard_map/psum | solution.py:90
  34.9 9.3 %all-to-all-done.2 = bf16[8,256,256]{1,2,0:T(8,128)(2,1)} async-done(((bf16[8,256,256]{1,2,0:T(8,128)(2,1)}), bf16[8,256,256]{1,2,0:T(8,128)(2,1)}, u32[]{:S(2)}, u32[]{:S(2)}) %all-to-all-start.2) | async-done | bytes 1048608 | tf_op jit(solution)/shard_map/all_to_all | solution.py:94
  54.4 24.1 %fusion.66 = bf16[8,273,256]{2,0,1:T(8,128)(2,1)S(1)} fusion(bf16[256,1,128]{0,1,2:T(2,128)(2,1)S(1)} %copy.126, bf16[1,7,127,256]{3,1,2,0:T(8,128)(2,1)S(1)} %slice.20, bf16[1,8,273,256]{3,1,2,0:T(8,128)(2,1)S(1)} %select_bitcast_fusion), kind=kOutput, calls=%fused_computation.86 | convolution fusion | flops 148604928 | bytes 2757120 | tf_op jit(solution)/shard_map/conv_general_dilated | solution.py:11
  96.1 6.0 %add_bitcast_fusion = (f32[256,32,128]{2,1,0:T(8,128)S(1)}, f32[256,32,128]{2,1,0:T(8,128)S(1)}, f32[256,32,128]{2,1,0:T(8,128)S(1)}, f32[256,32,128]{2,1,0:T(8,128)S(1)}) fusion(f32[32,256,128]{2,0,1:T(8,128)S(1)} %fusion.161, f32[32,128]{1,0:T(8,128)S(1)} %get-tuple-element.38, f32[32,128]{1,0:T(8,128)S(1)} %get-tuple-element.39, ...), kind=kOutput, calls=%fused_computation.24 | convolution fusion | flops 216013824 | bytes 30441472 | tf_op jit(solution)/shard_map/kn,cnq->ckq/dot_general | solution.py:54
  102.1 8.6 %fusion.12 = f32[256,32,128]{2,0,1:T(8,128)} fusion(f32[256,32,128]{2,1,0:T(8,128)S(1)} %get-tuple-element.29), kind=kOutput, calls=%fused_computation.29 | convolution fusion | flops 1610842112 | bytes 8388608 | tf_op jit(solution)/shard_map/ckq,qr->ckr/dot_general | solution.py:58
  110.7 6.8 %fusion.10 = f32[256,32,128]{2,0,1:T(8,128)S(1)} fusion(f32[256,32,128]{2,1,0:T(8,128)S(1)} %get-tuple-element.29), kind=kOutput, calls=%fused_computation.27 | convolution fusion | flops 1610842112 | bytes 8388608 | tf_op jit(solution)/shard_map/ckq,qr->ckr/dot_general | solution.py:61
  117.5 7.2 %fusion.18 = f32[256,32,128]{2,0,1:T(8,128)S(1)} fusion(f32[256,32,128]{2,1,0:T(8,128)S(1)} %get-tuple-element.36), kind=kOutput, calls=%fused_computation.35 | convolution fusion | flops 1610842112 | bytes 8388608 | tf_op jit(solution)/shard_map/ckq,qr->ckr/dot_general | solution.py:61
  124.7 7.1 %fusion.20 = f32[256,32,128]{2,0,1:T(8,128)S(1)} fusion(f32[256,32,128]{2,1,0:T(8,128)S(1)} %get-tuple-element.36), kind=kOutput, calls=%fused_computation.37 | convolution fusion | flops 1610842112 | bytes 8388608 | tf_op jit(solution)/shard_map/ckq,qr->ckr/dot_general | solution.py:58
  131.8 13.2 %fusion.92 = f32[256,32,128]{2,0,1:T(8,128)} fusion(f32[256,128,32]{1,2,0:T(8,128)S(1)} %copy-done.2, f32[256,128,32]{1,2,0:T(8,128)S(1)} %copy-done.3, f32[32,128]{1,0:T(8,128)S(1)} %get-tuple-element.38, f32[32,128]{1,0:T(8,128)S(1)} %get-tuple-element.39), kind=kOutput, calls=%fused_computation.109 | convolution fusion | flops 1615036416 | bytes 12615680 | tf_op jit(solution)/shard_map/ckq,qr->ckr/dot_general | solution.py:58
  145.0 12.9 %fusion.88 = f32[256,32,128]{2,0,1:T(8,128)} fusion(f32[256,128,32]{1,2,0:T(8,128)S(1)} %copy-done.2, f32[256,128,32]{1,2,0:T(8,128)S(1)} %copy-done.3, f32[32,128]{1,0:T(8,128)S(1)} %get-tuple-element.38, f32[32,128]{1,0:T(8,128)S(1)} %get-tuple-element.39), kind=kOutput, calls=%fused_computation.108 | convolution fusion | flops 1615036416 | bytes 12615680 | tf_op jit(solution)/shard_map/ckq,qr->ckr/dot_general | solution.py:61
  159.2 14.5 %convolution_add_fusion.1 = f32[256,32,128]{2,0,1:T(8,128)} fusion(f32[256,32,128]{2,0,1:T(8,128)} %fusion.92, f32[256,128,32]{1,2,0:T(8,128)S(1)} %copy-done.2, f32[256,128,32]{1,2,0:T(8,128)S(1)} %copy-done.3, f32[32,128]{1,0:T(8,128)S(1)} %get-tuple-element.38, f32[32,128]{1,0:T(8,128)S(1)} %get-tuple-element.39), kind=kOutput, calls=%fused_computation.62 | convolution fusion | flops 1616084992 | bytes 16809984 | tf_op jit(solution)/shard_map/ckq,qr->ckr/dot_general | solution.py:58
  173.7 8.4 %fusion.36 = f32[256,32,128]{2,0,1:T(8,128)} fusion(f32[256,32,128]{2,0,1:T(8,128)S(1)} %copy-done.8, f32[256,32,128]{2,1,0:T(8,128)S(1)} %get-tuple-element.28), kind=kOutput, calls=%fused_computation.57 | convolution fusion | flops 1611890688 | bytes 12582912 | tf_op jit(solution)/shard_map/ckq,qr->ckr/dot_general | solution.py:58
  182.1 8.6 %fusion.39 = f32[256,32,128]{2,0,1:T(8,128)} fusion(f32[256,32,128]{2,0,1:T(8,128)S(1)} %fusion.10, f32[256,32,128]{2,1,0:T(8,128)S(1)} %get-tuple-element.28), kind=kOutput, calls=%fused_computation.58 | convolution fusion | flops 1611890688 | bytes 12582912 | tf_op jit(solution)/shard_map/ckq,qr->ckr/dot_general | solution.py:61
  190.7 8.6 %fusion.33 = f32[256,32,128]{2,0,1:T(8,128)} fusion(f32[256,32,128]{2,0,1:T(8,128)S(1)} %fusion.18, f32[256,32,128]{2,1,0:T(8,128)S(1)} %get-tuple-element.37), kind=kOutput, calls=%fused_computation.56 | convolution fusion | flops 1611890688 | bytes 12582912 | tf_op jit(solution)/shard_map/ckq,qr->ckr/dot_general | solution.py:61
  199.3 8.4 %fusion.30 = f32[256,32,128]{2,0,1:T(8,128)} fusion(f32[256,32,128]{2,0,1:T(8,128)S(1)} %fusion.20, f32[256,32,128]{2,1,0:T(8,128)S(1)} %get-tuple-element.37), kind=kOutput, calls=%fused_computation.55 | convolution fusion | flops 1611890688 | bytes 12582912 | tf_op jit(solution)/shard_map/ckq,qr->ckr/dot_general | solution.py:58
  207.7 22.7 %multiply_subtract_fusion.1 = (f32[256,32,128]{2,0,1:T(8,128)}, f32[256,32,128]{2,0,1:T(8,128)}, f32[256,32,128]{2,0,1:T(8,128)}, f32[256,32,128]{2,0,1:T(8,128)}) fusion(f32[256,32,128]{2,0,1:T(8,128)} %fusion.36, f32[256,32,128]{2,0,1:T(8,128)} %convolution_add_fusion.1, f32[256,32,128]{2,0,1:T(8,128)} %fusion.39, f32[256,32,128]{2,0,1:T(8,128)} %fusion.33, ...), kind=kOutput, calls=%fused_computation.17 | convolution fusion | flops 1628667904 | bytes 50364416 | tf_op jit(solution)/shard_map/ckq,qr->ckr/dot_general | solution.py:61
  263.3 11.6 %multiply_subtract_fusion = (f32[256,32,128]{2,0,1:T(8,128)}, f32[256,32,128]{2,0,1:T(8,128)}, f32[256,32,128]{2,0,1:T(8,128)}, f32[256,32,128]{2,0,1:T(8,128)}) fusion(f32[256,32,128]{2,0,1:T(8,128)S(1)} %convolution_subtract_fusion, f32[32,128]{1,0:T(8,128)S(1)} %get-tuple-element.38, f32[32,128]{1,0:T(8,128)S(1)} %get-tuple-element.39, ...), kind=kOutput, calls=%fused_computation.16 | convolution fusion | flops 1624473600 | bytes 37781504 | tf_op jit(solution)/shard_map/ckq,qr->ckr/dot_general | solution.py:73
  274.9 7.0 %fusion.6 = f32[256,128,16]{1,2,0:T(8,128)S(1)} fusion(f32[256,32,128]{2,0,1:T(8,128)} %get-tuple-element.34), kind=kOutput, calls=%fused_computation.11 | convolution fusion | flops 201333760 | bytes 6291456 | tf_op jit(solution)/shard_map/kn,ckq->cnq/dot_general | solution.py:78
  289.9 28.6 %select_convert_fusion.1 = bf16[8,273,256]{2,0,1:T(8,128)(2,1)S(1)} fusion(bf16[256,1,128]{0,1,2:T(2,128)(2,1)S(1)} %copy-done.14, bf16[256,1,7,127]{0,2,3,1:T(8,128)(2,1)S(1)} %slice.16, bf16[256,1,8,273]{0,2,3,1:T(8,128)(2,1)S(1)} %copy.117, pred[8,273]{0,1:T(8,128)(4,1)S(1)} %copy-done.15), kind=kOutput, calls=%fused_computation.54 | convolution fusion | flops 149164032 | bytes 2759304 | tf_op jit(solution)/shard_map/conv_general_dilated | solution.py:11
  330.6 6.8 %fusion.2 = f32[256,128,16]{1,2,0:T(8,128)S(1)} fusion(f32[256,32,128]{2,0,1:T(8,128)} %get-tuple-element.25), kind=kOutput, calls=%fused_computation.6 | convolution fusion | flops 201333760 | bytes 6291456 | tf_op jit(solution)/shard_map/kn,ckq->cnq/dot_general | solution.py:78
  337.5 6.5 %reshape.129 = bf16[1,2184,256]{2,0,1:T(2,128)(2,1)} reshape(bf16[8,273,256]{2,1,0:T(8,128)(2,1)} %copy.133) | data formatting | bytes 2236416 | tf_op jit(solution)/shard_map/convert_element_type | solution.py:103
  349.9 25.4 %fusion.326 = f32[1,256,128]{1,0,2:T(1,128)S(1)} fusion(bf16[1,2184,256]{2,0,1:T(2,128)(2,1)} %reshape.129, bf16[256,1,2048]{0,1,2:T(2,128)(2,1)} %copy.135), kind=kOutput, calls=%fused_computation.326 | convolution fusion | flops 134217728 | bytes 2297856 | tf_op jit(solution)/shard_map/conv_general_dilated | solution.py:11
  380.3 6.9 %subtract_multiply_fusion = f32[256,128,16]{1,2,0:T(8,128)S(1)} fusion(f32[256,128,16]{1,2,0:T(8,128)S(1)} %fusion.2, f32[256,32,128]{2,0,1:T(8,128)} %get-tuple-element.24), kind=kOutput, calls=%fused_computation.72 | convolution fusion | flops 202382336 | bytes 8388608 | tf_op jit(solution)/shard_map/kn,ckq->cnq/dot_general | solution.py:78
  391.8 38.4 %fusion.42 = f32[1,256,7]{1,0,2:T(1,128)S(1)} fusion(bf16[1,256,2054]{1,2,0:T(8,128)(2,1)S(1)} %slice_bitcast_fusion.1, bf16[256,1,2048]{0,2,1:T(8,128)(2,1)S(1)} %slice_bitcast_fusion.2), kind=kOutput, calls=%fused_computation.65 | convolution fusion | flops 7340032 | bytes 2107392 | tf_op jit(solution)/shard_map/conv_general_dilated | solution.py:11
  (111 shorter events, 125.8 us)
Async XLA Ops:
  0.6 18.7 %copy-start = (bf16[2048,128]{1,0:T(8,128)(2,1)S(1)}, bf16[2048,128]{1,0:T(8,128)(2,1)}, u32[]{:S(2)}) copy-start(bf16[2048,128]{1,0:T(8,128)(2,1)} %param.9) | copy-start | bytes 1572868
  13.5 30.7 %all-to-all-start.2 = ((bf16[8,256,256]{1,2,0:T(8,128)(2,1)}), bf16[8,256,256]{1,2,0:T(8,128)(2,1)}, u32[]{:S(2)}, u32[]{:S(2)}) async-start(bf16[8,256,256]{1,2,0:T(8,128)(2,1)} %copy.122), calls=%async_computation.2 | async-start | bytes 2097152 | tf_op jit(solution)/shard_map/all_to_all | solution.py:94
  44.2 45.7 %all-to-all-start = ((bf16[8,256,256]{2,1,0:T(8,128)(2,1)}), bf16[8,256,256]{2,1,0:T(8,128)(2,1)}, u32[]{:S(2)}, u32[]{:S(2)}) async-start(bf16[8,256,256]{2,1,0:T(8,128)(2,1)} %bitcast.210), calls=%async_computation | async-start | bytes 2097152 | tf_op jit(solution)/shard_map/all_to_all | solution.py:95
  48.4 2.2 copy-start.16
  53.4 25.2 %copy-start.11 = (bf16[8,273,256]{2,0,1:T(8,128)(2,1)}, bf16[8,273,256]{2,0,1:T(8,128)(2,1)S(1)}, u32[]{:S(2)}) copy-start(bf16[8,273,256]{2,0,1:T(8,128)(2,1)S(1)} %select_convert_fusion) | copy-start | bytes 3354628
  92.8 3.3 copy-start.9
  124.7 7.1 %copy-start.2 = (f32[256,128,32]{1,2,0:T(8,128)S(1)}, f32[256,128,32]{1,2,0:T(8,128)}, u32[]{:S(2)}) copy-start(f32[256,128,32]{1,2,0:T(8,128)} %fusion.166) | copy-start | bytes 12582916
  124.7 7.1 %copy-start.3 = (f32[256,128,32]{1,2,0:T(8,128)S(1)}, f32[256,128,32]{1,2,0:T(8,128)}, u32[]{:S(2)}) copy-start(f32[256,128,32]{1,2,0:T(8,128)} %fusion.158) | copy-start | bytes 12582916
  145.0 12.9 %copy-start.12 = (bf16[8,273,256]{2,0,1:T(8,128)(2,1)S(1)}, bf16[8,273,256]{2,0,1:T(8,128)(2,1)}, u32[]{:S(2)}) copy-start(bf16[8,273,256]{2,0,1:T(8,128)(2,1)} %copy-done.11) | copy-start | bytes 3354628
  159.2 14.5 %copy-start.8 = (f32[256,32,128]{2,0,1:T(8,128)S(1)}, f32[256,32,128]{2,0,1:T(8,128)}, u32[]{:S(2)}) copy-start(f32[256,32,128]{2,0,1:T(8,128)} %fusion.12) | copy-start | bytes 12582916
  230.4 6.0 %copy-start.6 = (f32[256,32,128]{2,0,1:T(8,128)S(1)}, f32[256,32,128]{2,0,1:T(8,128)}, u32[]{:S(2)}) copy-start(f32[256,32,128]{2,0,1:T(8,128)} %get-tuple-element.20) | copy-start | bytes 12582916
  242.1 3.8 copy-start.4
  245.9 3.8 copy-start.5
  257.7 5.6 %copy-start.7 = (f32[256,32,128]{2,0,1:T(8,128)S(1)}, f32[256,32,128]{2,0,1:T(8,128)}, u32[]{:S(2)}) copy-start(f32[256,32,128]{2,0,1:T(8,128)} %get-tuple-element.21) | copy-start | bytes 12582916
  274.9 7.0 %copy-start.10 = (f32[256,32,128]{2,0,1:T(8,128)S(1)}, f32[256,32,128]{2,0,1:T(8,128)}, u32[]{:S(2)}) copy-start(f32[256,32,128]{2,0,1:T(8,128)} %get-tuple-element.35) | copy-start | bytes 12582916
  289.0 0.9 copy-start.14
  289.0 0.9 copy-start.15
  318.5 2.2 copy-start.17
  324.7 106.2 %all-to-all-start.1 = ((bf16[256,8,256]{0,2,1:T(8,128)(2,1)}), bf16[256,8,256]{0,2,1:T(8,128)(2,1)}, u32[]{:S(2)}, u32[]{:S(2)}) async-start(bf16[256,8,256]{0,2,1:T(8,128)(2,1)} %bitcast.19), calls=%async_computation.1 | async-start | bytes 2097152 | tf_op jit(solution)/shard_map/all_to_all | solution.py:126
  387.2 4.5 %copy-start.13 = (bf16[256,2054]{0,1:T(8,128)(2,1)S(1)}, bf16[256,2054]{0,1:T(8,128)(2,1)}, u32[]{:S(2)}) copy-start(bf16[256,2054]{0,1:T(8,128)(2,1)} %slice_bitcast_fusion) | copy-start | bytes 3154948
  391.8 41.4 %copy-start.1 = (bf16[2048,128]{1,0:T(8,128)(2,1)S(1)}, bf16[2048,128]{1,0:T(8,128)(2,1)}, u32[]{:S(2)}) copy-start(bf16[2048,128]{1,0:T(8,128)(2,1)} %param.9) | copy-start | bytes 1572868
where the time goes:
time: 440 us; the launch traced here: 434 us
  matrix products  346 us (79%)
  local copies, waits for them, and re-layouts  46.6 us (11%)
  starting transfers between devices  15.9 us (4%)
  waiting for transfers between devices  9.3 us (2%)
  blocking collectives  8.36 us (2%)
  other arithmetic  5.68 us (1%)
    conv_general_dilated x6, matrix products, depthwise(): lax.conv_general_dilated(signal[None], taps[:, None, :], (1,), 'VALID', d...  122 us
    dot_general x3, matrix products, forward_dft(): jnp.einsum('ckq,qr->ckr', turned_re, sin_inner, precision=highest)  39.9 us
    dot_general x3, matrix products, forward_dft(): jnp.einsum('ckq,qr->ckr', turned_im, sin_inner, precision=highest)  30.2 us
    dot_general x3, matrix products, forward_dft(): jnp.einsum('ckq,qr->ckr', turned_re, cos_inner, precision=highest)  30 us
    dot_general x3, matrix products, forward_dft(): jnp.einsum('ckq,qr->ckr', turned_im, cos_inner, precision=highest)  26.9 us
    dot_general x2, matrix products, inverse_dft(): jnp.einsum('ckq,qr->ckr', spec_re, sin_inner, precision=highest)  17.2 us
    dot_general x3, matrix products, forward_dft(): real = jnp.einsum('kn,cnq->ckq', cos_outer, blocks, precision=highest)  15 us
    dot_general x2, matrix products, inverse_dft(): jnp.einsum('kn,ckq->cnq', sin_outer, turned_im, precision=highest)  13.8 us
  transfers between devices with their start and end apart: 3, of which 1 were waited for; matrix products, arithmetic and copies ran while one was open for 36% of the time, Pallas kernels for 0%

commit v1 on v0

--- a/solution.py
+++ b/solution.py
@@ -3,6 +3,7 @@
 import jax.numpy as jnp
 from jax import lax
 from jax.sharding import PartitionSpec as P
+from jax.lax import axis_index, ppermute, psum
 
 highest = lax.Precision.HIGHEST
 
@@ -90,8 +91,25 @@
     squares = lax.psum(jnp.sum(inputs32 * inputs32, axis=0), "ch")
     inv_rms = lax.rsqrt(squares / (chans * lax.axis_size("ch")) + 1e-05)
     normed = (inputs32 * inv_rms[None, :] * norm_gain[:, None]).astype(jnp.bfloat16)
+
+    def space_take(shard_in, along_axis, dimension_no, out_dim):
+        raw_out, t1 = (psum(1, along_axis), axis_index(along_axis))
+        b_next = shard_in.shape[dimension_no] // raw_out
+        w2 = jnp.roll(shard_in, -t1 * b_next, dimension_no)
+        pile = [lax.slice_in_dim(w2, 0, b_next, axis=dimension_no)]
+        t = 1
+        while t < raw_out:
+            tile_out = lax.slice_in_dim(w2, t * b_next, (t + 1) * b_next, axis=dimension_no)
+            pile.append(
+                ppermute(tile_out, along_axis, [(dd, (dd + t) % raw_out) for dd in range(raw_out)])
+            )
+            t += 1
+        return jnp.roll(
+            jnp.concatenate(pile[::-1], out_dim), (t1 + 1) * pile[0].shape[out_dim], out_dim
+        )
+
     arrived, grad_chan = (
-        lax.all_to_all(normed, "seq", split_axis=0, concat_axis=1, tiled=True),
+        space_take(normed, "seq", 0, 1),
         lax.all_to_all(grad_out, "seq", split_axis=0, concat_axis=1, tiled=True),
     )
     group, length = arrived.shape

time: 440 us -> 427 us (0.970)
  starting transfers between devices: 15.9 us -> 30 us
  matrix products: 346 us -> 332 us
  local copies, waits for them, and re-layouts: 46.6 us -> 39.8 us
    ppermute x0 -> x7, starting transfers between devices: none -> 18.2 us  [space_take(): ppermute(tile_out, along_axis, [(dd, (dd + t) % raw_out) for dd in range(...]
    conv_general_dilated x6, matrix products: 122 us -> 112 us  [depthwise(): lax.conv_general_dilated(signal[None], taps[:, None, :], (1,), 'VALID', d...]
    all_to_all x1 -> x0, waiting for transfers between devices: 9.3 us -> none  [on_device(): lax.all_to_all(normed, 'seq', split_axis=0, concat_axis=1, tiled=True)]
    all_to_all x1 -> x0, starting transfers between devices: 5.81 us -> none  [on_device(): lax.all_to_all(normed, 'seq', split_axis=0, concat_axis=1, tiled=True)]
    ppermute x0 -> x7, waiting for transfers between devices: none -> 5.71 us  [space_take(): ppermute(tile_out, along_axis, [(dd, (dd + t) % raw_out) for dd in range(...]
    convert_element_type x4, local copies, waits for them, and re-layouts: 6.09 us -> 0.64 us  [on_device(): shorted_grad = depthwise(back_pad, medium_local).astype(jnp.bfloat16)]
  transfers between devices with their start and end apart: 3 -> 9, of which waited for: 1 -> 2; matrix products, arithmetic and copies ran while one was open for 36% -> 43% of each run, Pallas kernels for 0% -> 0%
where the time goes in v1:
time: 427 us; the launch traced here: 420 us
  matrix products  332 us (78%)
  local copies, waits for them, and re-layouts  39.8 us (9%)
  starting transfers between devices  30 us (7%)
  blocking collectives  6.73 us (2%)
  waiting for transfers between devices  5.72 us (1%)
    conv_general_dilated x6, matrix products, depthwise(): lax.conv_general_dilated(signal[None], taps[:, None, :], (1,), 'VALID', d...  112 us
    dot_general x3, matrix products, forward_dft(): jnp.einsum('ckq,qr->ckr', turned_re, sin_inner, precision=highest)  39.2 us
    dot_general x3, matrix products, forward_dft(): jnp.einsum('ckq,qr->ckr', turned_re, cos_inner, precision=highest)  31.5 us
    dot_general x3, matrix products, forward_dft(): jnp.einsum('ckq,qr->ckr', turned_im, cos_inner, precision=highest)  27.1 us
    dot_general x3, matrix products, forward_dft(): jnp.einsum('ckq,qr->ckr', turned_im, sin_inner, precision=highest)  27 us
    ppermute x7, starting transfers between devices, space_take(): ppermute(tile_out, along_axis, [(dd, (dd + t) % raw_out) for dd in range(...  18.2 us
    dot_general x2, matrix products, inverse_dft(): jnp.einsum('ckq,qr->ckr', spec_re, sin_inner, precision=highest)  17.1 us
    dot_general x3, matrix products, forward_dft(): real = jnp.einsum('kn,cnq->ckq', cos_outer, blocks, precision=highest)  15 us
  transfers between devices with their start and end apart: 9, of which 2 were waited for; matrix products, arithmetic and copies ran while one was open for 43% of the time, Pallas kernels for 0%

profile of v1, /device:TPU:0, one launch (start us, length us, event | category | flops | bytes accessed | tf_op | source)
XLA Modules:
  0.0 419.7 jit_solution(14141013815121735997)
XLA Ops:
  0.7 7.4 %all-to-all-start = ((bf16[8,256,256]{2,1,0:T(8,128)(2,1)}), bf16[8,256,256]{2,1,0:T(8,128)(2,1)}, u32[]{:S(2)}, u32[]{:S(2)}) async-start(bf16[8,256,256]{2,1,0:T(8,128)(2,1)} %bitcast.205), calls=%async_computation | async-start | bytes 2097152 | tf_op jit(solution)/shard_map/all_to_all | solution.py:113
  9.8 6.7 %psum.7 = f32[256]{0:T(256)S(1)} all-reduce(f32[256]{0:T(256)S(1)} %fusion.44), channel_id=1, replica_groups=mesh['seq'=8,'ch'=4] {'ch'}, use_global_device_ids=true, to_apply=%region_1.0 | all-reduce | flops 256 | bytes 2048 | tf_op jit(solution)/shard_map/psum | solution.py:91
  43.3 8.1 %collective-permute-start.6 = (bf16[256,256]{0,1:T(8,128)(2,1)S(1)}, bf16[256,256]{0,1:T(8,128)(2,1)S(1)}, u32[]{:S(2)}, u32[]{:S(2)}) collective-permute-start(bf16[256,256]{0,1:T(8,128)(2,1)S(1)} %get-tuple-element.34), channel_id=1, source_target_pairs={{0,4},{4,8},{8,12},{12,16},{16,20},{20,24},{24,28},{28,0},{1,5},{5... | collective-permute-start | bytes 393224 | tf_op jit(solution)/shard_map/ppermute | solution.py:104
  63.5 24.1 %fusion.66 = bf16[8,273,256]{2,0,1:T(8,128)(2,1)S(1)} fusion(bf16[256,1,128]{0,1,2:T(2,128)(2,1)S(1)} %copy.126, bf16[1,7,127,256]{3,1,2,0:T(8,128)(2,1)S(1)} %slice.60, bf16[1,8,273,256]{3,1,2,0:T(8,128)(2,1)S(1)} %select_bitcast_fusion), kind=kOutput, calls=%fused_computation.88 | convolution fusion | flops 148604928 | bytes 2757120 | tf_op jit(solution)/shard_map/conv_general_dilated | solution.py:12
  105.6 14.1 %fusion.93 = f32[256,32,128]{2,0,1:T(8,128)S(1)} fusion(f32[256,128,32]{1,2,0:T(8,128)} %fusion.167, f32[256,128,32]{1,2,0:T(8,128)} %fusion.159, f32[32,128]{1,0:T(8,128)S(1)} %get-tuple-element.45, f32[32,128]{1,0:T(8,128)S(1)} %get-tuple-element.46), kind=kOutput, calls=%fused_computation.112 | convolution fusion | flops 1615036416 | bytes 12615680 | tf_op jit(solution)/shard_map/ckq,qr->ckr/dot_general | solution.py:59
  119.8 12.9 %fusion.89 = f32[256,32,128]{2,0,1:T(8,128)} fusion(f32[256,128,32]{1,2,0:T(8,128)S(1)} %copy-done.2, f32[256,128,32]{1,2,0:T(8,128)S(1)} %copy-done.3, f32[32,128]{1,0:T(8,128)S(1)} %get-tuple-element.45, f32[32,128]{1,0:T(8,128)S(1)} %get-tuple-element.46), kind=kOutput, calls=%fused_computation.111 | convolution fusion | flops 1615036416 | bytes 12615680 | tf_op jit(solution)/shard_map/ckq,qr->ckr/dot_general | solution.py:62
  132.7 13.0 %convolution_add_fusion.1 = f32[256,32,128]{2,0,1:T(8,128)} fusion(f32[256,32,128]{2,0,1:T(8,128)S(1)} %fusion.93, f32[256,128,32]{1,2,0:T(8,128)S(1)} %copy-done.2, f32[256,128,32]{1,2,0:T(8,128)S(1)} %copy-done.3, f32[32,128]{1,0:T(8,128)S(1)} %get-tuple-element.45, f32[32,128]{1,0:T(8,128)S(1)} %get-tuple-element.46), kind=kOutput, calls=%fused_computation.62 | convolution fusion | flops 1616084992 | bytes 16809984 | tf_op jit(solution)/shard_map/ckq,qr->ckr/dot_general | solution.py:59
  152.4 6.0 %add_bitcast_fusion = (f32[256,32,128]{2,1,0:T(8,128)S(1)}, f32[256,32,128]{2,1,0:T(8,128)S(1)}, f32[256,32,128]{2,1,0:T(8,128)S(1)}, f32[256,32,128]{2,1,0:T(8,128)S(1)}) fusion(f32[32,256,128]{2,0,1:T(8,128)S(1)} %fusion.162, f32[32,128]{1,0:T(8,128)S(1)} %get-tuple-element.45, f32[32,128]{1,0:T(8,128)S(1)} %get-tuple-element.46, ...), kind=kOutput, calls=%fused_computation.24 | convolution fusion | flops 216013824 | bytes 30441472 | tf_op jit(solution)/shard_map/kn,cnq->ckq/dot_general | solution.py:55
  158.4 7.0 %fusion.12 = f32[256,32,128]{2,0,1:T(8,128)S(1)} fusion(f32[256,32,128]{2,1,0:T(8,128)S(1)} %get-tuple-element.29), kind=kOutput, calls=%fused_computation.29 | convolution fusion | flops 1610842112 | bytes 8388608 | tf_op jit(solution)/shard_map/ckq,qr->ckr/dot_general | solution.py:59
  165.4 7.0 %fusion.10 = f32[256,32,128]{2,0,1:T(8,128)S(1)} fusion(f32[256,32,128]{2,1,0:T(8,128)S(1)} %get-tuple-element.29), kind=kOutput, calls=%fused_computation.27 | convolution fusion | flops 1610842112 | bytes 8388608 | tf_op jit(solution)/shard_map/ckq,qr->ckr/dot_general | solution.py:62
  172.4 7.2 %fusion.18 = f32[256,32,128]{2,0,1:T(8,128)S(1)} fusion(f32[256,32,128]{2,1,0:T(8,128)S(1)} %get-tuple-element.43), kind=kOutput, calls=%fused_computation.35 | convolution fusion | flops 1610842112 | bytes 8388608 | tf_op jit(solution)/shard_map/ckq,qr->ckr/dot_general | solution.py:62
  179.6 7.0 %fusion.20 = f32[256,32,128]{2,0,1:T(8,128)S(1)} fusion(f32[256,32,128]{2,1,0:T(8,128)S(1)} %get-tuple-element.43), kind=kOutput, calls=%fused_computation.37 | convolution fusion | flops 1610842112 | bytes 8388608 | tf_op jit(solution)/shard_map/ckq,qr->ckr/dot_general | solution.py:59
  186.6 8.8 %fusion.36 = f32[256,32,128]{2,0,1:T(8,128)} fusion(f32[256,32,128]{2,0,1:T(8,128)S(1)} %fusion.12, f32[256,32,128]{2,1,0:T(8,128)S(1)} %get-tuple-element.28), kind=kOutput, calls=%fused_computation.57 | convolution fusion | flops 1611890688 | bytes 12582912 | tf_op jit(solution)/shard_map/ckq,qr->ckr/dot_general | solution.py:59
  195.3 8.5 %fusion.39 = f32[256,32,128]{2,0,1:T(8,128)} fusion(f32[256,32,128]{2,0,1:T(8,128)S(1)} %fusion.10, f32[256,32,128]{2,1,0:T(8,128)S(1)} %get-tuple-element.28), kind=kOutput, calls=%fused_computation.58 | convolution fusion | flops 1611890688 | bytes 12582912 | tf_op jit(solution)/shard_map/ckq,qr->ckr/dot_general | solution.py:62
  203.8 8.5 %fusion.33 = f32[256,32,128]{2,0,1:T(8,128)} fusion(f32[256,32,128]{2,0,1:T(8,128)S(1)} %fusion.18, f32[256,32,128]{2,1,0:T(8,128)S(1)} %get-tuple-element.44), kind=kOutput, calls=%fused_computation.56 | convolution fusion | flops 1611890688 | bytes 12582912 | tf_op jit(solution)/shard_map/ckq,qr->ckr/dot_general | solution.py:62
  212.3 8.6 %fusion.30 = f32[256,32,128]{2,0,1:T(8,128)} fusion(f32[256,32,128]{2,0,1:T(8,128)S(1)} %fusion.20, f32[256,32,128]{2,1,0:T(8,128)S(1)} %get-tuple-element.44), kind=kOutput, calls=%fused_computation.55 | convolution fusion | flops 1611890688 | bytes 12582912 | tf_op jit(solution)/shard_map/ckq,qr->ckr/dot_general | solution.py:59
  220.9 22.3 %multiply_subtract_fusion.1 = (f32[256,32,128]{2,0,1:T(8,128)}, f32[256,32,128]{2,0,1:T(8,128)}, f32[256,32,128]{2,0,1:T(8,128)}, f32[256,32,128]{2,0,1:T(8,128)}) fusion(f32[256,32,128]{2,0,1:T(8,128)} %fusion.36, f32[256,32,128]{2,0,1:T(8,128)} %convolution_add_fusion.1, f32[256,32,128]{2,0,1:T(8,128)} %fusion.39, f32[256,32,128]{2,0,1:T(8,128)} %fusion.33, ...), kind=kOutput, calls=%fused_computation.17 | convolution fusion | flops 1628667904 | bytes 50364416 | tf_op jit(solution)/shard_map/ckq,qr->ckr/dot_general | solution.py:62
  243.1 6.0 %fusion.112 = f32[256,32,128]{2,0,1:T(8,128)S(1)} fusion(f32[256,32,128]{2,0,1:T(8,128)} %get-tuple-element.21), kind=kOutput, calls=%fused_computation.136 | convolution fusion | flops 1610842112 | bytes 8388608 | tf_op jit(solution)/shard_map/ckq,qr->ckr/dot_general | solution.py:71
  276.0 11.6 %multiply_subtract_fusion = (f32[256,32,128]{2,0,1:T(8,128)}, f32[256,32,128]{2,0,1:T(8,128)}, f32[256,32,128]{2,0,1:T(8,128)}, f32[256,32,128]{2,0,1:T(8,128)}) fusion(f32[256,32,128]{2,0,1:T(8,128)S(1)} %convolution_subtract_fusion, f32[32,128]{1,0:T(8,128)S(1)} %get-tuple-element.45, f32[32,128]{1,0:T(8,128)S(1)} %get-tuple-element.46, ...), kind=kOutput, calls=%fused_computation.16 | convolution fusion | flops 1624473600 | bytes 37781504 | tf_op jit(solution)/shard_map/ckq,qr->ckr/dot_general | solution.py:74
  287.7 7.0 %fusion.6 = f32[256,128,16]{1,2,0:T(8,128)S(1)} fusion(f32[256,32,128]{2,0,1:T(8,128)} %get-tuple-element.41), kind=kOutput, calls=%fused_computation.11 | convolution fusion | flops 201333760 | bytes 6291456 | tf_op jit(solution)/shard_map/kn,ckq->cnq/dot_general | solution.py:79
  302.6 28.8 %select_convert_fusion.1 = bf16[8,273,256]{2,0,1:T(8,128)(2,1)S(1)} fusion(bf16[256,1,128]{0,1,2:T(2,128)(2,1)S(1)} %copy-done.12, bf16[256,1,7,127]{0,2,3,1:T(8,128)(2,1)S(1)} %slice.48, bf16[256,1,8,273]{0,2,3,1:T(8,128)(2,1)S(1)} %copy.117, pred[8,273]{0,1:T(8,128)(4,1)S(1)} %copy-done.13), kind=kOutput, calls=%fused_computation.54 | convolution fusion | flops 149164032 | bytes 2759304 | tf_op jit(solution)/shard_map/conv_general_dilated | solution.py:12
  343.1 7.0 %fusion.2 = f32[256,128,16]{1,2,0:T(8,128)S(1)} fusion(f32[256,32,128]{2,0,1:T(8,128)} %get-tuple-element.25), kind=kOutput, calls=%fused_computation.6 | convolution fusion | flops 201333760 | bytes 6291456 | tf_op jit(solution)/shard_map/kn,ckq->cnq/dot_general | solution.py:79
  361.0 25.4 %fusion.328 = f32[1,256,128]{1,0,2:T(1,128)S(1)} fusion(bf16[1,2184,256]{2,0,1:T(2,128)(2,1)} %reshape.126, bf16[256,1,2048]{0,1,2:T(2,128)(2,1)} %copy.135), kind=kOutput, calls=%fused_computation.347 | convolution fusion | flops 134217728 | bytes 2297856 | tf_op jit(solution)/shard_map/conv_general_dilated | solution.py:12
  388.0 28.6 %fusion.42 = f32[1,256,7]{1,0,2:T(1,128)S(1)} fusion(bf16[1,256,2054]{1,2,0:T(8,128)(2,1)} %slice_bitcast_fusion.1, bf16[256,1,2048]{0,2,1:T(8,128)(2,1)S(1)} %slice_bitcast_fusion.2), kind=kOutput, calls=%fused_computation.65 | convolution fusion | flops 7340032 | bytes 2107392 | tf_op jit(solution)/shard_map/conv_general_dilated | solution.py:12
  (140 shorter events, 126.5 us)
Async XLA Ops:
  0.6 37.3 %copy-start = (bf16[2048,128]{1,0:T(8,128)(2,1)S(1)}, bf16[2048,128]{1,0:T(8,128)(2,1)}, u32[]{:S(2)}) copy-start(bf16[2048,128]{1,0:T(8,128)(2,1)} %param.9) | copy-start | bytes 1572868
  0.6 15.9 %copy-start.15 = (f32[2048]{0:T(1024)S(1)}, f32[2048]{0:T(1024)}, u32[]{:S(2)}) copy-start(f32[2048]{0:T(1024)} %param.7) | copy-start | bytes 24580
  0.7 145.1 %all-to-all-start = ((bf16[8,256,256]{2,1,0:T(8,128)(2,1)}), bf16[8,256,256]{2,1,0:T(8,128)(2,1)}, u32[]{:S(2)}, u32[]{:S(2)}) async-start(bf16[8,256,256]{2,1,0:T(8,128)(2,1)} %bitcast.205), calls=%async_computation | async-start | bytes 2097152 | tf_op jit(solution)/shard_map/all_to_all | solution.py:113
  17.6 23.6 %collective-permute-start = (bf16[256,256]{0,1:T(8,128)(2,1)S(1)}, bf16[256,256]{0,1:T(8,128)(2,1)S(1)}, u32[]{:S(2)}, u32[]{:S(2)}) collective-permute-start(bf16[256,256]{0,1:T(8,128)(2,1)S(1)} %get-tuple-element.40), channel_id=1, source_target_pairs={{0,28},{4,0},{8,4},{12,8},{16,12},{20,16},{24,20},{28,24},{1,29},{... | collective-permute-start | bytes 393224 | tf_op jit(solution)/shard_map/ppermute | solution.py:104
  22.0 21.2 %collective-permute-start.1 = (bf16[256,256]{0,1:T(8,128)(2,1)S(1)}, bf16[256,256]{0,1:T(8,128)(2,1)S(1)}, u32[]{:S(2)}, u32[]{:S(2)}) collective-permute-start(bf16[256,256]{0,1:T(8,128)(2,1)S(1)} %get-tuple-element.39), channel_id=1, source_target_pairs={{0,24},{4,28},{8,0},{12,4},{16,8},{20,12},{24,16},{28,20},{1,25},{... | collective-permute-start | bytes 393224 | tf_op jit(solution)/shard_map/ppermute | solution.py:104
  22.6 28.8 %collective-permute-start.2 = (bf16[256,256]{0,1:T(8,128)(2,1)S(1)}, bf16[256,256]{0,1:T(8,128)(2,1)S(1)}, u32[]{:S(2)}, u32[]{:S(2)}) collective-permute-start(bf16[256,256]{0,1:T(8,128)(2,1)S(1)} %get-tuple-element.38), channel_id=1, source_target_pairs={{0,20},{4,24},{8,28},{12,0},{16,4},{20,8},{24,12},{28,16},{1,21},{... | collective-permute-start | bytes 393224 | tf_op jit(solution)/shard_map/ppermute | solution.py:104
  22.6 33.7 %collective-permute-start.3 = (bf16[256,256]{0,1:T(8,128)(2,1)S(1)}, bf16[256,256]{0,1:T(8,128)(2,1)S(1)}, u32[]{:S(2)}, u32[]{:S(2)}) collective-permute-start(bf16[256,256]{0,1:T(8,128)(2,1)S(1)} %get-tuple-element.37), channel_id=1, source_target_pairs={{0,16},{4,20},{8,24},{12,28},{16,0},{20,4},{24,8},{28,12},{1,17},{... | collective-permute-start | bytes 393224 | tf_op jit(solution)/shard_map/ppermute | solution.py:104
  25.1 32.0 %collective-permute-start.4 = (bf16[256,256]{0,1:T(8,128)(2,1)S(1)}, bf16[256,256]{0,1:T(8,128)(2,1)S(1)}, u32[]{:S(2)}, u32[]{:S(2)}) collective-permute-start(bf16[256,256]{0,1:T(8,128)(2,1)S(1)} %get-tuple-element.36), channel_id=1, source_target_pairs={{0,12},{4,16},{8,20},{12,24},{16,28},{20,0},{24,4},{28,8},{1,13},{... | collective-permute-start | bytes 393224 | tf_op jit(solution)/shard_map/ppermute | solution.py:104
  41.2 16.0 %collective-permute-start.5 = (bf16[256,256]{0,1:T(8,128)(2,1)S(1)}, bf16[256,256]{0,1:T(8,128)(2,1)S(1)}, u32[]{:S(2)}, u32[]{:S(2)}) collective-permute-start(bf16[256,256]{0,1:T(8,128)(2,1)S(1)} %get-tuple-element.35), channel_id=1, source_target_pairs={{0,8},{4,12},{8,16},{12,20},{16,24},{20,28},{24,0},{28,4},{1,9},{5... | collective-permute-start | bytes 393224 | tf_op jit(solution)/shard_map/ppermute | solution.py:104
  43.3 13.9 %collective-permute-start.6 = (bf16[256,256]{0,1:T(8,128)(2,1)S(1)}, bf16[256,256]{0,1:T(8,128)(2,1)S(1)}, u32[]{:S(2)}, u32[]{:S(2)}) collective-permute-start(bf16[256,256]{0,1:T(8,128)(2,1)S(1)} %get-tuple-element.34), channel_id=1, source_target_pairs={{0,4},{4,8},{8,12},{12,16},{16,20},{20,24},{24,28},{28,0},{1,5},{5... | collective-permute-start | bytes 393224 | tf_op jit(solution)/shard_map/ppermute | solution.py:104
  57.8 1.9 copy-start.14
  105.6 14.2 %copy-start.2 = (f32[256,128,32]{1,2,0:T(8,128)S(1)}, f32[256,128,32]{1,2,0:T(8,128)}, u32[]{:S(2)}) copy-start(f32[256,128,32]{1,2,0:T(8,128)} %fusion.167) | copy-start | bytes 12582916
  105.6 14.2 %copy-start.3 = (f32[256,128,32]{1,2,0:T(8,128)S(1)}, f32[256,128,32]{1,2,0:T(8,128)}, u32[]{:S(2)}) copy-start(f32[256,128,32]{1,2,0:T(8,128)} %fusion.159) | copy-start | bytes 12582916
  149.1 3.3 copy-start.8
  243.1 6.0 %copy-start.6 = (f32[256,32,128]{2,0,1:T(8,128)S(1)}, f32[256,32,128]{2,0,1:T(8,128)}, u32[]{:S(2)}) copy-start(f32[256,32,128]{2,0,1:T(8,128)} %get-tuple-element.20) | copy-start | bytes 12582916
  255.1 3.8 copy-start.4
  258.9 3.8 copy-start.5
  270.5 5.5 %copy-start.7 = (f32[256,32,128]{2,0,1:T(8,128)S(1)}, f32[256,32,128]{2,0,1:T(8,128)}, u32[]{:S(2)}) copy-start(f32[256,32,128]{2,0,1:T(8,128)} %get-tuple-element.21) | copy-start | bytes 12582916
  287.7 7.0 %copy-start.9 = (f32[256,32,128]{2,0,1:T(8,128)S(1)}, f32[256,32,128]{2,0,1:T(8,128)}, u32[]{:S(2)}) copy-start(f32[256,32,128]{2,0,1:T(8,128)} %get-tuple-element.42) | copy-start | bytes 12582916
  331.5 1.2 copy-start.16
  338.7 78.6 %all-to-all-start.1 = ((bf16[256,8,256]{0,2,1:T(8,128)(2,1)}), bf16[256,8,256]{0,2,1:T(8,128)(2,1)}, u32[]{:S(2)}, u32[]{:S(2)}) async-start(bf16[256,8,256]{0,2,1:T(8,128)(2,1)} %bitcast.19), calls=%async_computation.1 | async-start | bytes 2097152 | tf_op jit(solution)/shard_map/all_to_all | solution.py:144
  343.1 7.0 %copy-start.10 = (f32[256,32,128]{2,0,1:T(8,128)S(1)}, f32[256,32,128]{2,0,1:T(8,128)}, u32[]{:S(2)}) copy-start(f32[256,32,128]{2,0,1:T(8,128)} %get-tuple-element.24) | copy-start | bytes 12582916
  355.0 2.2 copy-start.11
  388.0 31.5 %copy-start.1 = (bf16[2048,128]{1,0:T(8,128)(2,1)S(1)}, bf16[2048,128]{1,0:T(8,128)(2,1)}, u32[]{:S(2)}) copy-start(bf16[2048,128]{1,0:T(8,128)(2,1)} %param.9) | copy-start | bytes 1572868
  (2 other events, 1.8 us)
